TPU v7x, 256 devices: a whole 4x4x8 slice. The times are simulated.
256 devices in a mesh: region: 16 (over z, x_lo), neuron: 16 (over x_hi, y, core).
Axes of the slice: x: 4 (x_hi: 2, x_lo: 2; x = x_hi * 2 + x_lo), y: 4, z: 8, core: 2. Of those that a mesh axis runs over, the one named last changes fastest.
Arguments:
- counts: bfloat16 [16, 20480, 4096], P('region', 'neuron'), may hold values from 0 to 3, as said below
- latents: bfloat16 [64, 4096], P(None, 'neuron'), may hold values from -5 to 5
- loadings: bfloat16 [16, 64, 20480], P('region', None, 'neuron'), may hold values from -0.75 to 0.75
- bias: float32 [16, 20480], P('region', 'neuron'), may hold values from -3 to 3
- delays: int32 [16, 64], P('region'), may hold values from 0 to 128
- recorded: int32 [16], P('region'), may hold values from 1024 to 4096, as said below
Outputs:
- grad_latents: float32 [64, 4096], P(None, 'neuron')
- grad_loadings: float32 [16, 64, 20480], P('region', None, 'neuron')
- grad_bias: float32 [16, 20480], P('region', 'neuron')
Inputs may be any that keep to these rules, and one draw needn't show every extreme that they name: At least one region is recorded over all 4096 bins. `counts`: whole numbers.
All inputs are finite; a program needn't handle non-finite values.
Results may differ from a plain program's by a relative error of at most 0.0021.
Values may be sent and summed in bfloat16 or wider, within the bound.
A program may use at most 64 MiB of HBM per device.

v0:
```python
import jax
import jax.numpy as jnp
from jax import lax
from jax.sharding import PartitionSpec as P


def move_rows(source, delay_row, levels, forward):
    current = source
    for level in range(levels):
        amount = 1 << level
        if forward:
            displaced = jnp.pad(current[:, :-amount], ((0, 0), (amount, 0)))
        else:
            displaced = jnp.pad(current[:, amount:], ((0, 0), (0, amount)))
        chosen = delay_row // amount % 2 == 1
        current = jnp.where(chosen[:, None], displaced, current)
    return current


def delay_rows(source, delay_row, offset, span):
    result = move_rows(source, delay_row, offset.bit_length(), True)
    return result[:, offset : offset + span]


def advance_rows(source, delay_row, span, largest):
    result = move_rows(source, delay_row, largest.bit_length(), False)
    return result[:, :span]


def per_device(counts, latents, loadings, bias, delays, recorded):
    count_rows = counts[0]
    load = loadings[0]
    bias_row = bias[0]
    delay_row = delays[0]
    length = recorded[0]
    width = latents.shape[1]
    total = count_rows.shape[1]
    reach = width // 2
    lat_count = latents.shape[0]
    neu_count = count_rows.shape[0]

    def accumulate(carry, piece, start):
        grad_load, grad_bias, grad_shift = carry
        span = piece.shape[1]
        observed = lax.dynamic_slice_in_dim(count_rows, start, span, 1).astype(jnp.float32)
        eta = lax.dot_general(
            load, piece, (((0,), (0,)), ((), ())), preferred_element_type=jnp.float32
        )
        eta = eta + bias_row[:, None]
        bins = start + jnp.arange(span, dtype=jnp.int32)
        resid = jnp.where((bins < length)[None, :], jnp.exp(eta) - observed, 0.0)
        resid_low = resid.astype(jnp.bfloat16)
        grad_load = grad_load + lax.dot_general(
            piece, resid_low, (((1,), (1,)), ((), ())), preferred_element_type=jnp.float32
        )
        grad_bias = grad_bias + jnp.sum(resid, axis=1)
        block = jnp.dot(load, resid_low, preferred_element_type=jnp.float32)
        grad_shift = lax.dynamic_update_slice_in_dim(grad_shift, block, start, 1)
        return (grad_load, grad_bias, grad_shift)

    initial = (
        jnp.zeros((lat_count, neu_count), jnp.float32),
        jnp.zeros((neu_count,), jnp.float32),
        jnp.zeros((lat_count, total), jnp.float32),
    )
    whole = lax.all_gather(latents, "neuron", axis=1, tiled=True)
    shifted = delay_rows(jnp.pad(whole, ((0, 0), (reach, 0))), delay_row, reach, total)

    def visit(step, carry):
        begin = (step * width).astype(jnp.int32)
        return accumulate(carry, lax.dynamic_slice_in_dim(shifted, begin, width, 1), begin)

    grad_load, grad_bias, grad_shift = lax.fori_loop(0, total // width, visit, initial)
    source = advance_rows(jnp.pad(grad_shift, ((0, 0), (0, reach))), delay_row, total, reach)
    summed = lax.psum_scatter(source, "neuron", scatter_dimension=1, tiled=True)
    grad_latents = lax.psum(summed, "region")
    return (grad_latents, grad_load[None], grad_bias[None])


def solution(mesh):
    placed = (
        P("region", "neuron", None),
        P(None, "neuron"),
        P("region", None, "neuron"),
        P("region", "neuron"),
        P("region", None),
        P("region"),
    )
    return jax.shard_map(
        per_device,
        mesh=mesh,
        in_specs=placed,
        out_specs=(P(None, "neuron"), P("region", None, "neuron"), P("region", "neuron")),
        check_vma=False,
    )
```

profile of v0, /device:TPU:8, one launch (start us, length us, event | category | flops | bytes accessed | tf_op | source)
XLA Modules:
  0.0 316.7 jit_solution(13940699881098271327)
XLA Ops:
  7.2 0.7 fusion.11
  7.9 22.8 %all_gather.3 = bf16[64,4096]{1,0:T(8,128)(2,1)S(1)} all-gather(bf16[64,256]{1,0:T(8,128)(2,1)} %param.9), channel_id=1, replica_groups=mesh['region'=16,'neuron'=16] {'neuron'}, dimensions={1}, use_global_device_ids=true | all-gather | bytes 557056 | tf_op jit(solution)/shard_map/all_gather | solution.py:66
  32.7 14.5 %copy.9 = bf16[1,1280,4096]{1,2,0:T(8,128)(2,1)} copy(bf16[1,1280,4096]{2,1,0:T(8,128)(2,1)} %param.8) | data formatting | bytes 20971520 | tf_op args[0]
  47.4 0.7 copy-done.1
  48.1 47.3 %while.18 = (s32[]{:T(128)}, f32[64,1280]{1,0:T(8,128)S(1)}, f32[1280]{0:T(1024)S(1)}, f32[64,4096]{1,0:T(8,128)S(1)}, bf16[64,4096]{1,0:T(8,128)(2,1)S(1)}, /*i...) while((s32[]{:T(128)}, f32[64,1280]{1,0:T(8,128)S(1)}, ...), condition=%wide.region_2.3_spmd.clone, body=%wide.region_0.2_spmd.clone.sunk | while | flops 127960832 | bytes 3776474 | solution.py:73
  48.8 1.6 fusion.44
  51.7 1.6 fusion.44
  54.7 1.6 fusion.44
  56.9 0.7 add_compare_fusion.2
  57.6 1.6 fusion.44
  59.9 0.7 add_compare_fusion.2
  60.6 1.6 fusion.44
  63.5 1.6 fusion.44
  66.5 1.6 fusion.44
  68.7 0.7 add_compare_fusion.2
  69.5 1.6 fusion.44
  71.7 0.7 add_compare_fusion.2
  72.4 1.6 fusion.44
  75.4 1.6 fusion.44
  78.3 1.6 fusion.44
  80.6 0.7 add_compare_fusion.2
  81.3 1.6 fusion.44
  83.5 0.7 add_compare_fusion.2
  84.3 1.6 fusion.44
  87.2 1.6 fusion.44
  90.2 1.6 fusion.44
  92.4 0.7 add_compare_fusion.2
  93.1 1.6 fusion.44
  99.3 1.2 slice_select_fusion
  100.6 76.1 %reduce-scatter.2.cloned.1.call-done = f32[64,256]{1,0:T(8,128)} async-done(((f32[64,4096]{1,0:T(8,128)}), f32[64,256]{1,0:T(8,128)}) %reduce-scatter.2.cloned.1.call-update) | async-done | bytes 65552 | tf_op jit(solution)/shard_map/reduce_scatter | solution.py:75
  177.3 131.1 %all-reduce.20.cloned.1.call-done = f32[64,256]{1,0:T(8,128)} async-done(((f32[64,256]{1,0:T(8,128)}), f32[64,256]{1,0:T(8,128)}) %all-reduce.20.cloned.1.call-update) | async-done | bytes 65552 | tf_op jit(solution)/shard_map/psum | solution.py:76
  308.4 1.5 copy.24
  (111 shorter events, 22.4 us)
Async XLA Ops:
  7.2 169.5 %reduce-scatter.2.cloned.1.call-start = ((), (), s32[]{:S(2)}) async-start(), calls=%async_computation.1 | async-start | bytes 1114112 | tf_op jit(solution)/shard_map/reduce_scatter | solution.py:75
  47.2 0.9 copy-start.1
  47.2 0.9 copy-start.2
  95.4 0.8 copy-start
  100.6 207.8 %all-reduce.20.cloned.1.call-start = ((), (), s32[]{:S(2)}) async-start(), calls=%async_computation.2 | async-start | bytes 131072 | tf_op jit(solution)/shard_map/psum | solution.py:76
Sparse Core Ops, SparseCore 0:
  100.7 75.9 reduce-scatter.1
  179.5 128.8 all-reduce.19
where the time goes:
time: 318 us; the launch traced here: 317 us
  waiting for transfers between devices  207 us (65%)
  matrix products  35.2 us (11%)
  blocking collectives  22.8 us (7%)
  local copies, waits for them, and re-layouts  20.1 us (6%)
  other arithmetic  16.5 us (5%)
  between operations  14.2 us (4%)
    psum x1, waiting for transfers between devices, per_device(): grad_latents = lax.psum(summed, 'region')  131 us
    reduce_scatter x1, waiting for transfers between devices, per_device(): summed = lax.psum_scatter(source, 'neuron', scatter_dimension=1, tiled=True)  76.1 us
    dot_general x16, matrix products, accumulate(): lax.dot_general(load, piece, (((0,), (0,)), ((), ())), preferred_element_...  26.2 us
    all_gather x1, blocking collectives, per_device(): whole = lax.all_gather(latents, 'neuron', axis=1, tiled=True)  22.8 us
    unnamed x8, local copies, waits for them, and re-layouts  16.9 us
    lt x16, other arithmetic, accumulate(): resid = jnp.where((bins < length)[None, :], jnp.exp(eta) - observed, 0.0)  10.9 us
  transfers between devices with their start and end apart: 2, of which 2 were waited for; matrix products, arithmetic and copies ran while one was open for 0% of the time, Pallas kernels for 0%

commit v1 on v0

--- a/solution.py
+++ b/solution.py
@@ -63,7 +63,9 @@
         jnp.zeros((neu_count,), jnp.float32),
         jnp.zeros((lat_count, total), jnp.float32),
     )
-    whole = lax.all_gather(latents, "neuron", axis=1, tiled=True)
+    whole = jnp.concatenate(
+        lax.all_to_all(jnp.stack([latents] * lax.axis_size("neuron")), "neuron", 0, 0), axis=1
+    )
     shifted = delay_rows(jnp.pad(whole, ((0, 0), (reach, 0))), delay_row, reach, total)
 
     def visit(step, carry):

time: 318 us -> 305 us (0.959)
  blocking collectives: 22.8 us -> 0 us
  starting transfers between devices: 0.08 us -> 7.47 us
    all_gather x1 -> x0, blocking collectives: 22.8 us -> none  [per_device(): whole = lax.all_gather(latents, 'neuron', axis=1, tiled=True)]
    all_to_all x0 -> x1, starting transfers between devices: none -> 7.39 us  [per_device(): lax.all_to_all(jnp.stack([latents] * lax.axis_size('neuron')), 'neuron',...]
    unnamed x8 -> x10, local copies, waits for them, and re-layouts: 16.9 us -> 16.7 us
  transfers between devices with their start and end apart: 2 -> 3, of which waited for: 2 -> 2; matrix products, arithmetic and copies ran while one was open for 0% -> 5% of each run, Pallas kernels for 0% -> 0%
where the time goes in v1:
time: 305 us; the launch traced here: 303 us
  waiting for transfers between devices  208 us (68%)
  matrix products  35.3 us (12%)
  local copies, waits for them, and re-layouts  21.6 us (7%)
  other arithmetic  15.8 us (5%)
  between operations  14.2 us (5%)
  starting transfers between devices  7.47 us (2%)
    psum x1, waiting for transfers between devices, per_device(): grad_latents = lax.psum(summed, 'region')  131 us
    reduce_scatter x1, waiting for transfers between devices, per_device(): summed = lax.psum_scatter(source, 'neuron', scatter_dimension=1, tiled=True)  77 us
    dot_general x16, matrix products, accumulate(): lax.dot_general(load, piece, (((0,), (0,)), ((), ())), preferred_element_...  26.3 us
    unnamed x10, local copies, waits for them, and re-layouts  16.7 us
    lt x16, other arithmetic, accumulate(): resid = jnp.where((bins < length)[None, :], jnp.exp(eta) - observed, 0.0)  10.9 us
    all_to_all x1, starting transfers between devices, per_device(): lax.all_to_all(jnp.stack([latents] * lax.axis_size('neuron')), 'neuron',...  7.39 us
  transfers between devices with their start and end apart: 3, of which 2 were waited for; matrix products, arithmetic and copies ran while one was open for 5% of the time, Pallas kernels for 0%

profile of v1, /device:TPU:8, one launch (start us, length us, event | category | flops | bytes accessed | tf_op | source)
XLA Modules:
  0.0 303.1 jit_solution(8787796566576457615)
XLA Ops:
  7.2 1.6 stack.2
  8.8 7.4 %all-to-all-start = ((bf16[16,64,256]{2,1,0:T(8,128)(2,1)}), bf16[16,64,256]{2,1,0:T(8,128)(2,1)S(1)}, u32[]{:S(2)}, u32[]{:S(2)}) async-start(bf16[16,64,256]{2,1,0:T(8,128)(2,1)} %stack.2), calls=%async_computation | async-start | bytes 1048576 | tf_op jit(solution)/shard_map/all_to_all | solution.py:67
  16.2 14.3 %copy.12 = bf16[1,1280,4096]{1,2,0:T(8,128)(2,1)} copy(bf16[1,1280,4096]{2,1,0:T(8,128)(2,1)} %param.8) | data formatting | bytes 20971520 | tf_op args[0]
  32.9 0.7 copy-done.1
  33.6 47.4 %while.18 = (s32[]{:T(128)}, f32[64,1280]{1,0:T(8,128)S(1)}, f32[1280]{0:T(1024)S(1)}, f32[64,4096]{1,0:T(8,128)S(1)}, bf16[64,4096]{1,0:T(8,128)(2,1)S(1)}, /*i...) while((s32[]{:T(128)}, f32[64,1280]{1,0:T(8,128)S(1)}, ...), condition=%wide.region_2.3_spmd.clone, body=%wide.region_0.2_spmd.clone.sunk | while | flops 127960832 | bytes 3776474 | solution.py:75
  34.3 1.6 fusion.44
  37.3 1.6 fusion.44
  40.2 1.7 fusion.44
  42.5 0.7 add_compare_fusion.2
  43.2 1.7 fusion.44
  45.4 0.7 add_compare_fusion.2
  46.2 1.6 fusion.44
  49.1 1.6 fusion.44
  52.1 1.7 fusion.44
  54.3 0.7 add_compare_fusion.2
  55.0 1.7 fusion.44
  57.3 0.7 add_compare_fusion.2
  58.0 1.6 fusion.44
  61.0 1.6 fusion.44
  63.9 1.7 fusion.44
  66.2 0.7 add_compare_fusion.2
  66.9 1.7 fusion.44
  69.2 0.7 add_compare_fusion.2
  69.9 1.6 fusion.44
  72.8 1.6 fusion.44
  75.8 1.7 fusion.44
  78.0 0.7 add_compare_fusion.2
  78.8 1.7 fusion.44
  85.0 1.2 slice_select_fusion
  86.2 77.0 %reduce-scatter.2.cloned.1.call-done = f32[64,256]{1,0:T(8,128)} async-done(((f32[64,4096]{1,0:T(8,128)}), f32[64,256]{1,0:T(8,128)}) %reduce-scatter.2.cloned.1.call-update) | async-done | bytes 65552 | tf_op jit(solution)/shard_map/reduce_scatter | solution.py:77
  163.9 131.0 %all-reduce.20.cloned.1.call-done = f32[64,256]{1,0:T(8,128)} async-done(((f32[64,256]{1,0:T(8,128)}), f32[64,256]{1,0:T(8,128)}) %all-reduce.20.cloned.1.call-update) | async-done | bytes 65552 | tf_op jit(solution)/shard_map/psum | solution.py:78
  294.8 1.5 copy.28
  (116 shorter events, 22.5 us)
Async XLA Ops:
  8.8 21.8 %all-to-all-start = ((bf16[16,64,256]{2,1,0:T(8,128)(2,1)}), bf16[16,64,256]{2,1,0:T(8,128)(2,1)S(1)}, u32[]{:S(2)}, u32[]{:S(2)}) async-start(bf16[16,64,256]{2,1,0:T(8,128)(2,1)} %stack.2), calls=%async_computation | async-start | bytes 1048576 | tf_op jit(solution)/shard_map/all_to_all | solution.py:67
  16.2 147.1 %reduce-scatter.2.cloned.1.call-start = ((), (), s32[]{:S(2)}) async-start(), calls=%async_computation.2 | async-start | bytes 1114112 | tf_op jit(solution)/shard_map/reduce_scatter | solution.py:77
  16.2 14.3 %copy-start.3 = (s32[1,64]{1,0:T(1,128)S(1)}, s32[1,64]{1,0:T(1,128)}, u32[]{:S(2)}) copy-start(s32[1,64]{1,0:T(1,128)} %param.12) | copy-start | bytes 772
  32.7 0.9 copy-start.1
  32.7 0.9 copy-start.2
  81.0 0.8 copy-start
  86.2 208.7 %all-reduce.20.cloned.1.call-start = ((), (), s32[]{:S(2)}) async-start(), calls=%async_computation.3 | async-start | bytes 131072 | tf_op jit(solution)/shard_map/psum | solution.py:78
Sparse Core Ops, SparseCore 0:
  86.3 76.9 reduce-scatter.1
  166.0 128.7 all-reduce.19

commit v2 on v0

--- a/solution.py
+++ b/solution.py
@@ -73,7 +73,7 @@
     grad_load, grad_bias, grad_shift = lax.fori_loop(0, total // width, visit, initial)
     source = advance_rows(jnp.pad(grad_shift, ((0, 0), (0, reach))), delay_row, total, reach)
     summed = lax.psum_scatter(source, "neuron", scatter_dimension=1, tiled=True)
-    grad_latents = lax.psum(summed, "region")
+    grad_latents = jnp.sum(lax.all_gather(summed, "region"), axis=0)
     return (grad_latents, grad_load[None], grad_bias[None])
 
 

time: 318 us -> 257 us (0.81)
  waiting for transfers between devices: 207 us -> 145 us
    psum x1 -> x0, waiting for transfers between devices: 131 us -> none  [per_device(): grad_latents = lax.psum(summed, 'region')]
    all_gather x0 -> x1, waiting for transfers between devices: none -> 69.3 us  [per_device(): grad_latents = jnp.sum(lax.all_gather(summed, 'region'), axis=0)]
    unnamed x8 -> x7, local copies, waits for them, and re-layouts: 16.9 us -> 15.4 us
where the time goes in v2:
time: 257 us; the launch traced here: 255 us
  waiting for transfers between devices  145 us (56%)
  matrix products  35.2 us (14%)
  blocking collectives  22.8 us (9%)
  local copies, waits for them, and re-layouts  18.6 us (7%)
  other arithmetic  18.4 us (7%)
  between operations  14.2 us (6%)
    reduce_scatter x1, waiting for transfers between devices, per_device(): summed = lax.psum_scatter(source, 'neuron', scatter_dimension=1, tiled=True)  76.1 us
    all_gather x1, waiting for transfers between devices, per_device(): grad_latents = jnp.sum(lax.all_gather(summed, 'region'), axis=0)  69.3 us
    dot_general x16, matrix products, accumulate(): lax.dot_general(load, piece, (((0,), (0,)), ((), ())), preferred_element_...  26.2 us
    all_gather x1, blocking collectives, per_device(): whole = lax.all_gather(latents, 'neuron', axis=1, tiled=True)  22.8 us
    unnamed x7, local copies, waits for them, and re-layouts  15.4 us
    lt x16, other arithmetic, accumulate(): resid = jnp.where((bins < length)[None, :], jnp.exp(eta) - observed, 0.0)  10.9 us
  transfers between devices with their start and end apart: 2, of which 2 were waited for; matrix products, arithmetic and copies ran while one was open for 0% of the time, Pallas kernels for 0%

profile of v2, /device:TPU:8, one launch (start us, length us, event | category | flops | bytes accessed | tf_op | source)
XLA Modules:
  0.0 255.4 jit_solution(5036521654585094453)
XLA Ops:
  7.2 0.7 fusion.11
  7.9 22.8 %all_gather.9 = bf16[64,4096]{1,0:T(8,128)(2,1)S(1)} all-gather(bf16[64,256]{1,0:T(8,128)(2,1)} %param.9), channel_id=1, replica_groups=mesh['region'=16,'neuron'=16] {'neuron'}, dimensions={1}, use_global_device_ids=true | all-gather | bytes 557056 | tf_op jit(solution)/shard_map/all_gather | solution.py:66
  32.7 14.5 %copy.9 = bf16[1,1280,4096]{1,2,0:T(8,128)(2,1)} copy(bf16[1,1280,4096]{2,1,0:T(8,128)(2,1)} %param.8) | data formatting | bytes 20971520 | tf_op args[0]
  47.4 0.7 copy-done.1
  48.1 47.3 %while.18 = (s32[]{:T(128)}, f32[64,1280]{1,0:T(8,128)S(1)}, f32[1280]{0:T(1024)S(1)}, f32[64,4096]{1,0:T(8,128)S(1)}, bf16[64,4096]{1,0:T(8,128)(2,1)S(1)}, /*i...) while((s32[]{:T(128)}, f32[64,1280]{1,0:T(8,128)S(1)}, ...), condition=%wide.region_2.3_spmd.clone, body=%wide.region_0.2_spmd.clone.sunk | while | flops 127960832 | bytes 3776474 | solution.py:73
  48.8 1.6 fusion.44
  51.7 1.6 fusion.44
  54.7 1.6 fusion.44
  56.9 0.7 add_compare_fusion.2
  57.6 1.6 fusion.44
  59.9 0.7 add_compare_fusion.2
  60.6 1.6 fusion.44
  63.5 1.6 fusion.44
  66.5 1.6 fusion.44
  68.7 0.7 add_compare_fusion.2
  69.5 1.6 fusion.44
  71.7 0.7 add_compare_fusion.2
  72.4 1.6 fusion.44
  75.4 1.6 fusion.44
  78.3 1.6 fusion.44
  80.6 0.7 add_compare_fusion.2
  81.3 1.6 fusion.44
  83.5 0.7 add_compare_fusion.2
  84.3 1.6 fusion.44
  87.2 1.6 fusion.44
  90.2 1.6 fusion.44
  92.4 0.7 add_compare_fusion.2
  93.1 1.6 fusion.44
  99.3 1.2 slice_select_fusion
  100.6 76.1 %reduce-scatter.2.cloned.1.call-done = f32[64,256]{1,0:T(8,128)} async-done(((f32[64,4096]{1,0:T(8,128)}), f32[64,256]{1,0:T(8,128)}) %reduce-scatter.2.cloned.1.call-update) | async-done | bytes 65552 | tf_op jit(solution)/shard_map/reduce_scatter | solution.py:75
  177.3 69.3 %all-gather.3.cloned.1.call-done = f32[1024,256]{1,0:T(8,128)} async-done(((f32[64,256]{1,0:T(8,128)}), f32[1024,256]{1,0:T(8,128)}) %all-gather.3.cloned.1.call-update) | async-done | bytes 1048592 | tf_op jit(solution)/shard_map/all_gather | solution.py:76
  246.6 1.9 reduce_sum.22
  (111 shorter events, 22.4 us)
Async XLA Ops:
  7.2 169.5 %reduce-scatter.2.cloned.1.call-start = ((), (), s32[]{:S(2)}) async-start(), calls=%async_computation.1 | async-start | bytes 1114112 | tf_op jit(solution)/shard_map/reduce_scatter | solution.py:75
  47.2 0.9 copy-start.1
  47.2 0.9 copy-start.2
  95.4 0.8 copy-start
  100.6 146.1 %all-gather.3.cloned.1.call-start = ((), (), s32[]{:S(2)}) async-start(), calls=%async_computation.2 | async-start | bytes 1114112 | tf_op jit(solution)/shard_map/all_gather | solution.py:76
Sparse Core Ops, SparseCore 0:
  100.7 75.9 reduce-scatter.1
  178.6 67.9 all-gather.2
